TPU v7x, 512 devices: a whole 4x8x8 slice. The times are simulated.
512 devices in a mesh: loop: 16 (over y, x_hi), dp: 32 (over z, x_lo, core).
Axes of the slice: x: 4 (x_hi: 2, x_lo: 2; x = x_hi * 2 + x_lo), y: 8, z: 8, core: 2. Of those that a mesh axis runs over, the one named last changes fastest.
Arguments:
- images: bfloat16 [32, 32, 16, 16, 768], P('dp', 'loop'), may hold values from -6 to 6
- kernel: float32 [7, 7, 768], replicated, may hold values from -0.875 to 0.875
- ln_gain: float32 [768], replicated, may hold values from 0.5 to 1.5
- w_up: bfloat16 [768, 1536], P('dp'), may hold values from -0.21875 to 0.21875
- b_up: float32 [1536], replicated, may hold values from -3 to 3
- w_down: bfloat16 [1536, 768], P('dp'), may hold values from -0.15625 to 0.15625
- layer_scale: float32 [768], replicated, may hold values from 0.3 to 1
- w_head: bfloat16 [768, 1152], P('dp'), may hold values from -0.21875 to 0.21875
- text_rows: bfloat16 [32, 32, 1152], P('dp', 'loop'), may hold values from -6 to 6
- pair_ids: int32 [32, 32], P('dp', 'loop'), may hold values from 0 to 31, each once within a row
- log_temp: float32 [1], replicated, may hold values from 1.5 to 2.5
- loss_bias: float32 [1], replicated, may hold values from -6 to -2
Outputs:
- kernel_grad: float32 [7, 7, 768], replicated
- up_grad: float32 [768, 1536], P('dp')
- text_grad: float32 [32, 32, 1152], P('dp', 'loop')
Inputs may be any that keep to these rules, and one draw needn't show every extreme that they name: Each row of pair_ids holds every index of its group once.
All inputs are finite; a program needn't handle non-finite values.
Results may differ from a plain program's by a relative error of at most 0.04.
Values may be sent and summed in bfloat16 or wider, within the bound.
A program may use at most 64 MiB of HBM per device.

v0:
```python
import jax
import jax.numpy as jnp
from jax import lax
from jax.sharding import PartitionSpec as P

epsilon = 1e-06


def passed_along(value, axis, steps):
    count = lax.axis_size(axis)
    pairs = [(source, (source + steps) % count) for source in range(count)]
    return lax.ppermute(value, axis, pairs)


def image_tower(kernel, w_up, images, ln_gain, b_up, w_down, layer_scale, w_head):
    image_count = images.shape[0]
    grid_side = images.shape[1]
    channels = images.shape[3]
    padded = jnp.pad(images, ((0, 0), (3, 3), (3, 3), (0, 0)))
    conv_out = jnp.zeros(images.shape, jnp.float32)
    for row_off in range(7):
        for col_off in range(7):
            window = padded[:, row_off : row_off + grid_side, col_off : col_off + grid_side, :]
            conv_out = conv_out + window.astype(jnp.float32) * kernel[row_off, col_off]
    chan_mean = jnp.mean(conv_out, axis=-1, keepdims=True)
    centered = conv_out - chan_mean
    chan_var = jnp.mean(centered * centered, axis=-1, keepdims=True)
    normed = (centered * lax.rsqrt(chan_var + epsilon) * ln_gain).astype(jnp.bfloat16)
    flat_rows = normed.reshape(-1, channels)
    hidden = jnp.dot(flat_rows, w_up, preferred_element_type=jnp.float32) + b_up
    active = jax.nn.gelu(hidden, approximate=True).astype(jnp.bfloat16)
    mlp_out = jnp.dot(active, w_down, preferred_element_type=jnp.float32)
    block_out = images.reshape(-1, channels).astype(jnp.float32) + layer_scale * mlp_out
    pooled = jnp.mean(
        block_out.reshape(image_count, grid_side * grid_side, channels), axis=1
    ).astype(jnp.bfloat16)
    embedding = jnp.dot(pooled, w_head, preferred_element_type=jnp.float32)
    return embedding * lax.rsqrt(jnp.sum(embedding * embedding, axis=-1, keepdims=True) + epsilon)


def pair_grad(image_emb, text_emb, pair_row, text_index, logit_scale, logit_bias, group_size):
    logits = (
        logit_scale * jnp.dot(image_emb, text_emb.T, precision=lax.Precision.HIGHEST) + logit_bias
    )
    sign_of = jnp.where(pair_row[:, None] == text_index[None, :], 1.0, -1.0)
    return -sign_of * jax.nn.sigmoid(-sign_of * logits) / group_size


def body(
    images,
    kernel,
    ln_gain,
    w_up,
    b_up,
    w_down,
    layer_scale,
    w_head,
    text_rows,
    pair_ids,
    log_temp,
    loss_bias,
):
    loop_size = lax.axis_size("loop")
    loop_index = lax.axis_index("loop")
    up_full, down_full, head_full = (
        lax.all_gather(w_up, "dp", axis=0, tiled=True),
        lax.all_gather(w_down, "dp", axis=0, tiled=True),
        lax.all_gather(w_head, "dp", axis=0, tiled=True),
    )
    pictures = images[0]
    pair_row = pair_ids[0]
    img_dev = pictures.shape[0]
    group_size = img_dev * loop_size
    logit_scale = jnp.exp(log_temp[0])
    logit_bias = loss_bias[0]

    def run_tower(kernel_arg, up_arg):
        return image_tower(
            kernel_arg, up_arg, pictures, ln_gain, b_up, down_full, layer_scale, head_full
        )

    image_emb, pullback = jax.vjp(run_tower, kernel, up_full)
    raw_rows = text_rows[0].astype(jnp.float32)
    text_norm = jnp.sqrt(jnp.sum(raw_rows * raw_rows, axis=-1, keepdims=True) + epsilon)
    text_hat = raw_rows / text_norm
    rounded = lax.optimization_barrier(text_hat.astype(jnp.bfloat16))
    local_index = jnp.arange(img_dev, dtype=jnp.int32)

    def cycle_step(step_index, state):
        text_block, partials, image_cot = state
        source = (loop_index - step_index) % loop_size
        text_index = source * img_dev + local_index
        pair_weight = pair_grad(
            image_emb, text_block, pair_row, text_index, logit_scale, logit_bias, group_size
        )
        image_cot = image_cot + logit_scale * jnp.dot(
            pair_weight, text_block, precision=lax.Precision.HIGHEST
        )
        partials = partials + logit_scale * jnp.dot(
            pair_weight.T, image_emb, precision=lax.Precision.HIGHEST
        )
        text_block, partials = passed_along((text_block, partials), "loop", 1)
        return (text_block, partials, image_cot)

    start = (
        rounded.astype(jnp.float32),
        jnp.zeros(raw_rows.shape, jnp.float32),
        jnp.zeros(image_emb.shape, jnp.float32),
    )
    _, text_cot, image_cot = lax.fori_loop(0, loop_size, cycle_step, start)
    text_grad = (
        text_cot - text_hat * jnp.sum(text_hat * text_cot, axis=-1, keepdims=True)
    ) / text_norm
    kernel_part, up_part = pullback(image_cot)
    kernel_grad = lax.psum(kernel_part, ("loop", "dp"))
    up_rows = lax.psum_scatter(
        up_part.astype(jnp.float32).astype(jnp.bfloat16), "dp", scatter_dimension=0, tiled=True
    )
    up_grad = lax.psum(up_rows, "loop").astype(jnp.float32)
    return (kernel_grad, up_grad, text_grad[None])


def solution(mesh):
    placed = (
        P("dp", "loop", None, None, None),
        P(),
        P(),
        P("dp", None),
        P(),
        P("dp", None),
        P(),
        P("dp", None),
        P("dp", "loop", None),
        P("dp", "loop"),
        P(),
        P(),
    )
    return jax.shard_map(
        body,
        mesh=mesh,
        in_specs=placed,
        out_specs=(P(), P("dp", None), P("dp", "loop", None)),
        check_vma=False,
    )
```

profile of v0, /device:TPU:1, one launch (start us, length us, event | category | flops | bytes accessed | tf_op | source)
XLA Modules:
  0.0 996.5 jit_solution(3485320233537033907)
XLA Ops:
  15.5 30.5 %fusion.140 = (f32[2,16,16]{2,1,0:T(8,128)S(1)}, f32[2,16,16,768]{3,2,1,0:T(8,128)S(1)}) fusion(f32[768]{0:T(1024)S(1)} %get-tuple-element.377, f32[768]{0:T(1024)S(1)} %get-tuple-element.378, f32[768]{0:T(1024)S(1)} %get-tuple-element.331, f32[768]{0:T(1024)S(1)} %get-tuple-element.332, f32[768]{0:T(1024)S(1)} %get-tuple-element.333, ...), kind=kLoop, calls=%fused_computation.374 | loop fusion | flops 57802240 | bytes 2511872 | tf_op jit(solution)/shard_map/jvp()/reduce_sum | solution.py:25
  46.7 37.7 %all-gather.4.cloned.1.call-done = bf16[768,1536]{1,0:T(8,128)(2,1)} async-done(((bf16[24,1536]{1,0:T(8,128)(2,1)}), bf16[768,1536]{1,0:T(8,128)(2,1)}) %all-gather.4.cloned.1.call-update) | async-done | bytes 2359312 | tf_op jit(solution)/shard_map/all_gather | solution.py:66
  84.4 4.8 convolution_add_fusion
  89.2 65.1 %all-gather.6.cloned.1.call-done = bf16[1536,768]{1,0:T(8,128)(2,1)} async-done(((bf16[48,768]{1,0:T(8,128)(2,1)}), bf16[1536,768]{1,0:T(8,128)(2,1)}) %all-gather.6.cloned.1.call-update) | async-done | bytes 2359312 | tf_op jit(solution)/shard_map/all_gather | solution.py:67
  154.3 4.6 bitcast_reduce_fusion
  158.9 64.5 %all-gather.8.cloned.1.call-done = bf16[768,1152]{1,0:T(8,128)(2,1)} async-done(((bf16[24,1152]{1,0:T(8,128)(2,1)}), bf16[768,1152]{1,0:T(8,128)(2,1)}) %all-gather.8.cloned.1.call-update) | async-done | bytes 1769488 | tf_op jit(solution)/shard_map/all_gather | solution.py:68
  225.4 184.7 %while.20 = (s32[]{:T(128)}, f32[2,1152]{1,0:T(2,128)S(1)}, f32[2,1152]{1,0:T(2,128)S(1)}, f32[2,1152]{1,0:T(2,128)S(1)}, f32[]{:T(128)}, /*index=5*/s32[1,2]{1,...) while((s32[]{:T(128)}, f32[2,1152]{1,0:T(2,128)S(1)}, ...), condition=%wide.region_6.7_spmd.clone, body=%wide.region_5.6_spmd.clone.sunk | while | flops 177470 | bytes 166336 | solution.py:110
  225.5 4.3 collective-permute-start
  234.5 4.4 collective-permute-done.1
  242.0 4.6 collective-permute-start.1
  257.3 4.4 collective-permute-done.1
  264.8 4.6 collective-permute-start.1
  280.0 4.4 collective-permute-done.1
  287.5 4.6 collective-permute-start.1
  299.1 5.2 collective-permute-start.1
  311.4 6.0 collective-permute-start.1
  319.4 3.9 collective-permute-start
  324.4 3.9 collective-permute-start.1
  328.5 4.0 collective-permute-done.1
  339.6 4.1 collective-permute-done.1
  350.7 4.1 collective-permute-done.1
  361.8 4.1 collective-permute-done.1
  372.8 4.1 collective-permute-done.1
  384.0 4.0 collective-permute-done.1
  395.0 4.1 collective-permute-done.1
  402.2 4.1 collective-permute-start.1
  412.6 4.6 fusion.14
  426.0 5.0 fusion.117
  434.9 3.9 fusion.118
  440.1 119.1 %reduce-scatter.2.cloned.1.call-done = bf16[24,1536]{1,0:T(8,128)(2,1)} async-done(((bf16[768,1536]{1,0:T(8,128)(2,1)}), bf16[24,1536]{1,0:T(8,128)(2,1)}) %reduce-scatter.2.cloned.1.call-update) | async-done | bytes 73744 | tf_op jit(solution)/shard_map/reduce_scatter | solution.py:116
  560.5 148.9 %all-reduce.55.cloned.1.call-done = bf16[24,1536]{1,0:T(8,128)(2,1)} async-done(((bf16[24,1536]{1,0:T(8,128)(2,1)}), bf16[24,1536]{1,0:T(8,128)(2,1)}) %all-reduce.55.cloned.1.call-update) | async-done | bytes 73744 | tf_op jit(solution)/shard_map/psum | solution.py:119
  711.0 277.1 %all-reduce.53.cloned.1.call-done = f32[7,7,768]{2,1,0:T(8,128)} async-done(((f32[7,7,768]{2,1,0:T(8,128)}), f32[7,7,768]{2,1,0:T(8,128)}) %all-reduce.53.cloned.1.call-update) | async-done | bytes 150544 | tf_op jit(solution)/shard_map/psum | solution.py:115
  (232 shorter events, 131.4 us)
Async XLA Ops:
  7.2 77.2 %all-gather.4.cloned.1.call-start = ((), (), s32[]{:S(2)}) async-start(), calls=%async_computation.1 | async-start | bytes 2433024 | tf_op jit(solution)/shard_map/all_gather | solution.py:66
  7.9 146.4 %all-gather.6.cloned.1.call-start = ((), (), s32[]{:S(2)}) async-start(), calls=%async_computation.2 | async-start | bytes 2433024 | tf_op jit(solution)/shard_map/all_gather | solution.py:67
  8.6 214.8 %all-gather.8.cloned.1.call-start = ((), (), s32[]{:S(2)}) async-start(), calls=%async_computation.3 | async-start | bytes 1824768 | tf_op jit(solution)/shard_map/all_gather | solution.py:68
  9.4 549.9 %reduce-scatter.2.cloned.1.call-start = ((), (), s32[]{:S(2)}) async-start(), calls=%async_computation.5 | async-start | bytes 2433024 | tf_op jit(solution)/shard_map/reduce_scatter | solution.py:116
  225.5 13.5 %collective-permute-start = (f32[2,1152]{1,0:T(2,128)S(1)}, f32[2,1152]{1,0:T(2,128)S(1)}, u32[]{:S(2)}, u32[]{:S(2)}) collective-permute-start(f32[2,1152]{1,0:T(2,128)S(1)} %copy.20), channel_id=1, source_target_pairs={{0,32},{32,64},{64,96},{96,128},{128,160},{160,192},{192,224},{224... | collective-permute-start | bytes 27656 | tf_op jit(solution)/shard_map/while/body/eval_jaxpr/ppermute | solution.py:12
  230.9 8.0 collective-permute-start.1
  239.0 11.1 %collective-permute-start = (f32[2,1152]{1,0:T(2,128)S(1)}, f32[2,1152]{1,0:T(2,128)S(1)}, u32[]{:S(2)}, u32[]{:S(2)}) collective-permute-start(f32[2,1152]{1,0:T(2,128)S(1)} %copy.20), channel_id=1, source_target_pairs={{0,32},{32,64},{64,96},{96,128},{128,160},{160,192},{192,224},{224... | collective-permute-start | bytes 27656 | tf_op jit(solution)/shard_map/while/body/eval_jaxpr/ppermute | solution.py:12
  242.0 8.0 collective-permute-start.1
  250.1 11.6 %collective-permute-start = (f32[2,1152]{1,0:T(2,128)S(1)}, f32[2,1152]{1,0:T(2,128)S(1)}, u32[]{:S(2)}, u32[]{:S(2)}) collective-permute-start(f32[2,1152]{1,0:T(2,128)S(1)} %copy.20), channel_id=1, source_target_pairs={{0,32},{32,64},{64,96},{96,128},{128,160},{160,192},{192,224},{224... | collective-permute-start | bytes 27656 | tf_op jit(solution)/shard_map/while/body/eval_jaxpr/ppermute | solution.py:12
  253.7 8.0 collective-permute-start.1
  261.7 11.1 %collective-permute-start = (f32[2,1152]{1,0:T(2,128)S(1)}, f32[2,1152]{1,0:T(2,128)S(1)}, u32[]{:S(2)}, u32[]{:S(2)}) collective-permute-start(f32[2,1152]{1,0:T(2,128)S(1)} %copy.20), channel_id=1, source_target_pairs={{0,32},{32,64},{64,96},{96,128},{128,160},{160,192},{192,224},{224... | collective-permute-start | bytes 27656 | tf_op jit(solution)/shard_map/while/body/eval_jaxpr/ppermute | solution.py:12
  264.8 8.0 collective-permute-start.1
  272.8 11.6 %collective-permute-start = (f32[2,1152]{1,0:T(2,128)S(1)}, f32[2,1152]{1,0:T(2,128)S(1)}, u32[]{:S(2)}, u32[]{:S(2)}) collective-permute-start(f32[2,1152]{1,0:T(2,128)S(1)} %copy.20), channel_id=1, source_target_pairs={{0,32},{32,64},{64,96},{96,128},{128,160},{160,192},{192,224},{224... | collective-permute-start | bytes 27656 | tf_op jit(solution)/shard_map/while/body/eval_jaxpr/ppermute | solution.py:12
  276.4 8.0 collective-permute-start.1
  284.4 11.1 %collective-permute-start = (f32[2,1152]{1,0:T(2,128)S(1)}, f32[2,1152]{1,0:T(2,128)S(1)}, u32[]{:S(2)}, u32[]{:S(2)}) collective-permute-start(f32[2,1152]{1,0:T(2,128)S(1)} %copy.20), channel_id=1, source_target_pairs={{0,32},{32,64},{64,96},{96,128},{128,160},{160,192},{192,224},{224... | collective-permute-start | bytes 27656 | tf_op jit(solution)/shard_map/while/body/eval_jaxpr/ppermute | solution.py:12
  287.5 8.0 collective-permute-start.1
  295.5 11.6 %collective-permute-start = (f32[2,1152]{1,0:T(2,128)S(1)}, f32[2,1152]{1,0:T(2,128)S(1)}, u32[]{:S(2)}, u32[]{:S(2)}) collective-permute-start(f32[2,1152]{1,0:T(2,128)S(1)} %copy.20), channel_id=1, source_target_pairs={{0,32},{32,64},{64,96},{96,128},{128,160},{160,192},{192,224},{224... | collective-permute-start | bytes 27656 | tf_op jit(solution)/shard_map/while/body/eval_jaxpr/ppermute | solution.py:12
  299.1 8.0 collective-permute-start.1
  307.1 12.3 %collective-permute-start = (f32[2,1152]{1,0:T(2,128)S(1)}, f32[2,1152]{1,0:T(2,128)S(1)}, u32[]{:S(2)}, u32[]{:S(2)}) collective-permute-start(f32[2,1152]{1,0:T(2,128)S(1)} %copy.20), channel_id=1, source_target_pairs={{0,32},{32,64},{64,96},{96,128},{128,160},{160,192},{192,224},{224... | collective-permute-start | bytes 27656 | tf_op jit(solution)/shard_map/while/body/eval_jaxpr/ppermute | solution.py:12
  319.4 13.1 %collective-permute-start = (f32[2,1152]{1,0:T(2,128)S(1)}, f32[2,1152]{1,0:T(2,128)S(1)}, u32[]{:S(2)}, u32[]{:S(2)}) collective-permute-start(f32[2,1152]{1,0:T(2,128)S(1)} %copy.20), channel_id=1, source_target_pairs={{0,32},{32,64},{64,96},{96,128},{128,160},{160,192},{192,224},{224... | collective-permute-start | bytes 27656 | tf_op jit(solution)/shard_map/while/body/eval_jaxpr/ppermute | solution.py:12
  332.5 11.2 %collective-permute-start = (f32[2,1152]{1,0:T(2,128)S(1)}, f32[2,1152]{1,0:T(2,128)S(1)}, u32[]{:S(2)}, u32[]{:S(2)}) collective-permute-start(f32[2,1152]{1,0:T(2,128)S(1)} %copy.20), channel_id=1, source_target_pairs={{0,32},{32,64},{64,96},{96,128},{128,160},{160,192},{192,224},{224... | collective-permute-start | bytes 27656 | tf_op jit(solution)/shard_map/while/body/eval_jaxpr/ppermute | solution.py:12
  343.7 11.1 %collective-permute-start = (f32[2,1152]{1,0:T(2,128)S(1)}, f32[2,1152]{1,0:T(2,128)S(1)}, u32[]{:S(2)}, u32[]{:S(2)}) collective-permute-start(f32[2,1152]{1,0:T(2,128)S(1)} %copy.20), channel_id=1, source_target_pairs={{0,32},{32,64},{64,96},{96,128},{128,160},{160,192},{192,224},{224... | collective-permute-start | bytes 27656 | tf_op jit(solution)/shard_map/while/body/eval_jaxpr/ppermute | solution.py:12
  354.7 11.1 %collective-permute-start = (f32[2,1152]{1,0:T(2,128)S(1)}, f32[2,1152]{1,0:T(2,128)S(1)}, u32[]{:S(2)}, u32[]{:S(2)}) collective-permute-start(f32[2,1152]{1,0:T(2,128)S(1)} %copy.20), channel_id=1, source_target_pairs={{0,32},{32,64},{64,96},{96,128},{128,160},{160,192},{192,224},{224... | collective-permute-start | bytes 27656 | tf_op jit(solution)/shard_map/while/body/eval_jaxpr/ppermute | solution.py:12
  365.8 11.1 %collective-permute-start = (f32[2,1152]{1,0:T(2,128)S(1)}, f32[2,1152]{1,0:T(2,128)S(1)}, u32[]{:S(2)}, u32[]{:S(2)}) collective-permute-start(f32[2,1152]{1,0:T(2,128)S(1)} %copy.20), channel_id=1, source_target_pairs={{0,32},{32,64},{64,96},{96,128},{128,160},{160,192},{192,224},{224... | collective-permute-start | bytes 27656 | tf_op jit(solution)/shard_map/while/body/eval_jaxpr/ppermute | solution.py:12
  368.9 8.0 collective-permute-start.1
  376.9 11.1 %collective-permute-start = (f32[2,1152]{1,0:T(2,128)S(1)}, f32[2,1152]{1,0:T(2,128)S(1)}, u32[]{:S(2)}, u32[]{:S(2)}) collective-permute-start(f32[2,1152]{1,0:T(2,128)S(1)} %copy.20), channel_id=1, source_target_pairs={{0,32},{32,64},{64,96},{96,128},{128,160},{160,192},{192,224},{224... | collective-permute-start | bytes 27656 | tf_op jit(solution)/shard_map/while/body/eval_jaxpr/ppermute | solution.py:12
  380.0 8.0 collective-permute-start.1
  388.0 11.1 %collective-permute-start = (f32[2,1152]{1,0:T(2,128)S(1)}, f32[2,1152]{1,0:T(2,128)S(1)}, u32[]{:S(2)}, u32[]{:S(2)}) collective-permute-start(f32[2,1152]{1,0:T(2,128)S(1)} %copy.20), channel_id=1, source_target_pairs={{0,32},{32,64},{64,96},{96,128},{128,160},{160,192},{192,224},{224... | collective-permute-start | bytes 27656 | tf_op jit(solution)/shard_map/while/body/eval_jaxpr/ppermute | solution.py:12
  399.1 11.1 %collective-permute-start = (f32[2,1152]{1,0:T(2,128)S(1)}, f32[2,1152]{1,0:T(2,128)S(1)}, u32[]{:S(2)}, u32[]{:S(2)}) collective-permute-start(f32[2,1152]{1,0:T(2,128)S(1)} %copy.20), channel_id=1, source_target_pairs={{0,32},{32,64},{64,96},{96,128},{128,160},{160,192},{192,224},{224... | collective-permute-start | bytes 27656 | tf_op jit(solution)/shard_map/while/body/eval_jaxpr/ppermute | solution.py:12
  402.2 8.0 collective-permute-start.1
  421.2 288.2 %all-reduce.55.cloned.1.call-start = ((), (), s32[]{:S(2)}) async-start(), calls=%async_computation.6 | async-start | bytes 147456 | tf_op jit(solution)/shard_map/psum | solution.py:119
  559.3 428.8 %all-reduce.53.cloned.1.call-start = ((), (), s32[]{:S(2)}) async-start(), calls=%async_computation.4 | async-start | bytes 344064 | tf_op jit(solution)/shard_map/psum | solution.py:115
  (13 other events, 326.9 us)
Sparse Core Ops, SparseCore 0:
  10.1 74.2 all-gather.3
  86.5 67.7 all-gather.5
  156.5 66.9 all-gather.7
  421.4 137.8 reduce-scatter.1
  562.0 147.3 all-reduce.54
  715.6 272.4 all-reduce.52
where the time goes:
time: 998 us; the launch traced here: 997 us
  waiting for transfers between devices  774 us (78%)
  starting transfers between devices  104 us (10%)
  other arithmetic  50 us (5%)
  matrix products  44.9 us (4%)
  between operations  15.4 us (2%)
    psum x1, waiting for transfers between devices, body(): kernel_grad = lax.psum(kernel_part, ('loop', 'dp'))  277 us
    psum x1, waiting for transfers between devices, body(): up_grad = lax.psum(up_rows, 'loop').astype(jnp.float32)  149 us
    reduce_scatter x1, waiting for transfers between devices, body(): lax.psum_scatter(up_part.astype(jnp.float32).astype(jnp.bfloat16), 'dp',...  119 us
    ppermute x32, starting transfers between devices, passed_along(): return lax.ppermute(value, axis, pairs)  104 us
    all_gather x1, waiting for transfers between devices, body(): lax.all_gather(w_down, 'dp', axis=0, tiled=True)  65.1 us
    all_gather x1, waiting for transfers between devices, body(): lax.all_gather(w_head, 'dp', axis=0, tiled=True)  64.5 us
    ppermute x32, waiting for transfers between devices, passed_along(): return lax.ppermute(value, axis, pairs)  59.5 us
    all_gather x1, waiting for transfers between devices, body(): lax.all_gather(w_up, 'dp', axis=0, tiled=True)  37.7 us
  transfers between devices with their start and end apart: 38, of which 22 were waited for; matrix products, arithmetic and copies ran while one was open for 9% of the time, Pallas kernels for 0%

commit v1 on v0

--- a/solution.py
+++ b/solution.py
@@ -112,7 +112,7 @@
         text_cot - text_hat * jnp.sum(text_hat * text_cot, axis=-1, keepdims=True)
     ) / text_norm
     kernel_part, up_part = pullback(image_cot)
-    kernel_grad = lax.psum(kernel_part, ("loop", "dp"))
+    kernel_grad = lax.psum(lax.psum(kernel_part, "dp"), "loop")
     up_rows = lax.psum_scatter(
         up_part.astype(jnp.float32).astype(jnp.bfloat16), "dp", scatter_dimension=0, tiled=True
     )

time: 998 us -> 1110 us (1.11)
  waiting for transfers between devices: 774 us -> 876 us
    psum x1 -> x2, waiting for transfers between devices: 277 us -> 378 us  [body(): kernel_grad = lax.psum(lax.psum(kernel_part, 'dp'), 'loop')]
  transfers between devices with their start and end apart: 38 -> 39, of which waited for: 22 -> 23; matrix products, arithmetic and copies ran while one was open for 9% -> 8% of each run, Pallas kernels for 0% -> 0%
where the time goes in v1:
time: 1110 us; the launch traced here: 1100 us
  waiting for transfers between devices  876 us (79%)
  starting transfers between devices  104 us (9%)
  other arithmetic  50.4 us (5%)
  matrix products  45 us (4%)
  between operations  15.4 us (1%)
    psum x2, waiting for transfers between devices, body(): kernel_grad = lax.psum(lax.psum(kernel_part, 'dp'), 'loop')  378 us
    psum x1, waiting for transfers between devices, body(): up_grad = lax.psum(up_rows, 'loop').astype(jnp.float32)  151 us
    reduce_scatter x1, waiting for transfers between devices, body(): lax.psum_scatter(up_part.astype(jnp.float32).astype(jnp.bfloat16), 'dp',...  119 us
    ppermute x32, starting transfers between devices, passed_along(): return lax.ppermute(value, axis, pairs)  104 us
    all_gather x1, waiting for transfers between devices, body(): lax.all_gather(w_down, 'dp', axis=0, tiled=True)  65.1 us
    all_gather x1, waiting for transfers between devices, body(): lax.all_gather(w_head, 'dp', axis=0, tiled=True)  64.5 us
    ppermute x32, waiting for transfers between devices, passed_along(): return lax.ppermute(value, axis, pairs)  59.3 us
    all_gather x1, waiting for transfers between devices, body(): lax.all_gather(w_up, 'dp', axis=0, tiled=True)  37.4 us
  transfers between devices with their start and end apart: 39, of which 23 were waited for; matrix products, arithmetic and copies ran while one was open for 8% of the time, Pallas kernels for 0%

profile of v1, /device:TPU:1, one launch (start us, length us, event | category | flops | bytes accessed | tf_op | source)
XLA Modules:
  0.0 1099.2 jit_solution(10667623232011399382)
XLA Ops:
  15.5 30.9 %fusion.140 = (f32[2,16,16]{2,1,0:T(8,128)S(1)}, f32[2,16,16,768]{3,2,1,0:T(8,128)S(1)}) fusion(f32[768]{0:T(1024)S(1)} %get-tuple-element.377, f32[768]{0:T(1024)S(1)} %get-tuple-element.378, f32[768]{0:T(1024)S(1)} %get-tuple-element.331, f32[768]{0:T(1024)S(1)} %get-tuple-element.332, f32[768]{0:T(1024)S(1)} %get-tuple-element.333, ...), kind=kLoop, calls=%fused_computation.374 | loop fusion | flops 57802240 | bytes 2511872 | tf_op jit(solution)/shard_map/jvp()/reduce_sum | solution.py:25
  47.0 37.4 %all-gather.4.cloned.1.call-done = bf16[768,1536]{1,0:T(8,128)(2,1)} async-done(((bf16[24,1536]{1,0:T(8,128)(2,1)}), bf16[768,1536]{1,0:T(8,128)(2,1)}) %all-gather.4.cloned.1.call-update) | async-done | bytes 2359312 | tf_op jit(solution)/shard_map/all_gather | solution.py:66
  84.4 4.8 convolution_add_fusion
  89.2 65.1 %all-gather.6.cloned.1.call-done = bf16[1536,768]{1,0:T(8,128)(2,1)} async-done(((bf16[48,768]{1,0:T(8,128)(2,1)}), bf16[1536,768]{1,0:T(8,128)(2,1)}) %all-gather.6.cloned.1.call-update) | async-done | bytes 2359312 | tf_op jit(solution)/shard_map/all_gather | solution.py:67
  154.3 4.6 bitcast_reduce_fusion
  158.9 64.5 %all-gather.8.cloned.1.call-done = bf16[768,1152]{1,0:T(8,128)(2,1)} async-done(((bf16[24,1152]{1,0:T(8,128)(2,1)}), bf16[768,1152]{1,0:T(8,128)(2,1)}) %all-gather.8.cloned.1.call-update) | async-done | bytes 1769488 | tf_op jit(solution)/shard_map/all_gather | solution.py:68
  225.5 184.7 %while.20 = (s32[]{:T(128)}, f32[2,1152]{1,0:T(2,128)S(1)}, f32[2,1152]{1,0:T(2,128)S(1)}, f32[2,1152]{1,0:T(2,128)S(1)}, f32[]{:T(128)}, /*index=5*/s32[1,2]{1,...) while((s32[]{:T(128)}, f32[2,1152]{1,0:T(2,128)S(1)}, ...), condition=%wide.region_6.7_spmd.clone, body=%wide.region_5.6_spmd.clone.sunk | while | flops 177470 | bytes 166336 | solution.py:110
  225.5 4.3 collective-permute-start
  234.6 4.4 collective-permute-done.1
  242.1 4.6 collective-permute-start.1
  257.3 4.4 collective-permute-done.1
  264.8 4.6 collective-permute-start.1
  280.0 4.4 collective-permute-done.1
  287.5 4.6 collective-permute-start.1
  299.1 5.2 collective-permute-start.1
  311.4 6.0 collective-permute-start.1
  319.4 3.9 collective-permute-start
  328.5 4.0 collective-permute-done.1
  339.6 4.0 collective-permute-done.1
  350.7 4.1 collective-permute-done.1
  361.8 4.1 collective-permute-done.1
  372.9 4.0 collective-permute-done.1
  384.0 4.0 collective-permute-done.1
  395.1 4.0 collective-permute-done.1
  402.2 4.1 collective-permute-start.1
  412.6 4.6 fusion.14
  426.0 5.0 fusion.117
  434.9 3.9 fusion.118
  440.2 119.0 %reduce-scatter.2.cloned.1.call-done = bf16[24,1536]{1,0:T(8,128)(2,1)} async-done(((bf16[768,1536]{1,0:T(8,128)(2,1)}), bf16[24,1536]{1,0:T(8,128)(2,1)}) %reduce-scatter.2.cloned.1.call-update) | async-done | bytes 73744 | tf_op jit(solution)/shard_map/reduce_scatter | solution.py:116
  559.4 217.3 %all-reduce.54.cloned.1.call-done = f32[7,7,768]{2,1,0:T(8,128)} async-done(((f32[7,7,768]{2,1,0:T(8,128)}), f32[7,7,768]{2,1,0:T(8,128)}) %all-reduce.54.cloned.1.call-update) | async-done | bytes 150544 | tf_op jit(solution)/shard_map/psum | solution.py:115
  777.5 150.7 %all-reduce.58.cloned.1.call-done = bf16[24,1536]{1,0:T(8,128)(2,1)} async-done(((bf16[24,1536]{1,0:T(8,128)(2,1)}), bf16[24,1536]{1,0:T(8,128)(2,1)}) %all-reduce.58.cloned.1.call-update) | async-done | bytes 73744 | tf_op jit(solution)/shard_map/psum | solution.py:119
  929.7 161.0 %all-reduce.56.cloned.1.call-done = f32[7,7,768]{2,1,0:T(8,128)} async-done(((f32[7,7,768]{2,1,0:T(8,128)}), f32[7,7,768]{2,1,0:T(8,128)}) %all-reduce.56.cloned.1.call-update) | async-done | bytes 150544 | tf_op jit(solution)/shard_map/psum | solution.py:115
  (235 shorter events, 135.0 us)
Async XLA Ops:
  7.2 77.2 %all-gather.4.cloned.1.call-start = ((), (), s32[]{:S(2)}) async-start(), calls=%async_computation.1 | async-start | bytes 2433024 | tf_op jit(solution)/shard_map/all_gather | solution.py:66
  7.9 146.4 %all-gather.6.cloned.1.call-start = ((), (), s32[]{:S(2)}) async-start(), calls=%async_computation.2 | async-start | bytes 2433024 | tf_op jit(solution)/shard_map/all_gather | solution.py:67
  8.6 214.8 %all-gather.8.cloned.1.call-start = ((), (), s32[]{:S(2)}) async-start(), calls=%async_computation.3 | async-start | bytes 1824768 | tf_op jit(solution)/shard_map/all_gather | solution.py:68
  9.4 549.9 %reduce-scatter.2.cloned.1.call-start = ((), (), s32[]{:S(2)}) async-start(), calls=%async_computation.6 | async-start | bytes 2433024 | tf_op jit(solution)/shard_map/reduce_scatter | solution.py:116
  225.5 13.5 %collective-permute-start = (f32[2,1152]{1,0:T(2,128)S(1)}, f32[2,1152]{1,0:T(2,128)S(1)}, u32[]{:S(2)}, u32[]{:S(2)}) collective-permute-start(f32[2,1152]{1,0:T(2,128)S(1)} %copy.20), channel_id=1, source_target_pairs={{0,32},{32,64},{64,96},{96,128},{128,160},{160,192},{192,224},{224... | collective-permute-start | bytes 27656 | tf_op jit(solution)/shard_map/while/body/eval_jaxpr/ppermute | solution.py:12
  231.0 8.0 collective-permute-start.1
  239.0 11.1 %collective-permute-start = (f32[2,1152]{1,0:T(2,128)S(1)}, f32[2,1152]{1,0:T(2,128)S(1)}, u32[]{:S(2)}, u32[]{:S(2)}) collective-permute-start(f32[2,1152]{1,0:T(2,128)S(1)} %copy.20), channel_id=1, source_target_pairs={{0,32},{32,64},{64,96},{96,128},{128,160},{160,192},{192,224},{224... | collective-permute-start | bytes 27656 | tf_op jit(solution)/shard_map/while/body/eval_jaxpr/ppermute | solution.py:12
  242.1 8.0 collective-permute-start.1
  250.1 11.6 %collective-permute-start = (f32[2,1152]{1,0:T(2,128)S(1)}, f32[2,1152]{1,0:T(2,128)S(1)}, u32[]{:S(2)}, u32[]{:S(2)}) collective-permute-start(f32[2,1152]{1,0:T(2,128)S(1)} %copy.20), channel_id=1, source_target_pairs={{0,32},{32,64},{64,96},{96,128},{128,160},{160,192},{192,224},{224... | collective-permute-start | bytes 27656 | tf_op jit(solution)/shard_map/while/body/eval_jaxpr/ppermute | solution.py:12
  253.7 8.0 collective-permute-start.1
  261.7 11.1 %collective-permute-start = (f32[2,1152]{1,0:T(2,128)S(1)}, f32[2,1152]{1,0:T(2,128)S(1)}, u32[]{:S(2)}, u32[]{:S(2)}) collective-permute-start(f32[2,1152]{1,0:T(2,128)S(1)} %copy.20), channel_id=1, source_target_pairs={{0,32},{32,64},{64,96},{96,128},{128,160},{160,192},{192,224},{224... | collective-permute-start | bytes 27656 | tf_op jit(solution)/shard_map/while/body/eval_jaxpr/ppermute | solution.py:12
  264.8 8.0 collective-permute-start.1
  272.8 11.6 %collective-permute-start = (f32[2,1152]{1,0:T(2,128)S(1)}, f32[2,1152]{1,0:T(2,128)S(1)}, u32[]{:S(2)}, u32[]{:S(2)}) collective-permute-start(f32[2,1152]{1,0:T(2,128)S(1)} %copy.20), channel_id=1, source_target_pairs={{0,32},{32,64},{64,96},{96,128},{128,160},{160,192},{192,224},{224... | collective-permute-start | bytes 27656 | tf_op jit(solution)/shard_map/while/body/eval_jaxpr/ppermute | solution.py:12
  276.4 8.0 collective-permute-start.1
  284.4 11.1 %collective-permute-start = (f32[2,1152]{1,0:T(2,128)S(1)}, f32[2,1152]{1,0:T(2,128)S(1)}, u32[]{:S(2)}, u32[]{:S(2)}) collective-permute-start(f32[2,1152]{1,0:T(2,128)S(1)} %copy.20), channel_id=1, source_target_pairs={{0,32},{32,64},{64,96},{96,128},{128,160},{160,192},{192,224},{224... | collective-permute-start | bytes 27656 | tf_op jit(solution)/shard_map/while/body/eval_jaxpr/ppermute | solution.py:12
  287.5 8.0 collective-permute-start.1
  295.5 11.6 %collective-permute-start = (f32[2,1152]{1,0:T(2,128)S(1)}, f32[2,1152]{1,0:T(2,128)S(1)}, u32[]{:S(2)}, u32[]{:S(2)}) collective-permute-start(f32[2,1152]{1,0:T(2,128)S(1)} %copy.20), channel_id=1, source_target_pairs={{0,32},{32,64},{64,96},{96,128},{128,160},{160,192},{192,224},{224... | collective-permute-start | bytes 27656 | tf_op jit(solution)/shard_map/while/body/eval_jaxpr/ppermute | solution.py:12
  299.1 8.0 collective-permute-start.1
  307.2 12.2 %collective-permute-start = (f32[2,1152]{1,0:T(2,128)S(1)}, f32[2,1152]{1,0:T(2,128)S(1)}, u32[]{:S(2)}, u32[]{:S(2)}) collective-permute-start(f32[2,1152]{1,0:T(2,128)S(1)} %copy.20), channel_id=1, source_target_pairs={{0,32},{32,64},{64,96},{96,128},{128,160},{160,192},{192,224},{224... | collective-permute-start | bytes 27656 | tf_op jit(solution)/shard_map/while/body/eval_jaxpr/ppermute | solution.py:12
  311.4 8.0 collective-permute-start.1
  319.4 13.1 %collective-permute-start = (f32[2,1152]{1,0:T(2,128)S(1)}, f32[2,1152]{1,0:T(2,128)S(1)}, u32[]{:S(2)}, u32[]{:S(2)}) collective-permute-start(f32[2,1152]{1,0:T(2,128)S(1)} %copy.20), channel_id=1, source_target_pairs={{0,32},{32,64},{64,96},{96,128},{128,160},{160,192},{192,224},{224... | collective-permute-start | bytes 27656 | tf_op jit(solution)/shard_map/while/body/eval_jaxpr/ppermute | solution.py:12
  332.5 11.2 %collective-permute-start = (f32[2,1152]{1,0:T(2,128)S(1)}, f32[2,1152]{1,0:T(2,128)S(1)}, u32[]{:S(2)}, u32[]{:S(2)}) collective-permute-start(f32[2,1152]{1,0:T(2,128)S(1)} %copy.20), channel_id=1, source_target_pairs={{0,32},{32,64},{64,96},{96,128},{128,160},{160,192},{192,224},{224... | collective-permute-start | bytes 27656 | tf_op jit(solution)/shard_map/while/body/eval_jaxpr/ppermute | solution.py:12
  343.7 11.1 %collective-permute-start = (f32[2,1152]{1,0:T(2,128)S(1)}, f32[2,1152]{1,0:T(2,128)S(1)}, u32[]{:S(2)}, u32[]{:S(2)}) collective-permute-start(f32[2,1152]{1,0:T(2,128)S(1)} %copy.20), channel_id=1, source_target_pairs={{0,32},{32,64},{64,96},{96,128},{128,160},{160,192},{192,224},{224... | collective-permute-start | bytes 27656 | tf_op jit(solution)/shard_map/while/body/eval_jaxpr/ppermute | solution.py:12
  354.8 11.1 %collective-permute-start = (f32[2,1152]{1,0:T(2,128)S(1)}, f32[2,1152]{1,0:T(2,128)S(1)}, u32[]{:S(2)}, u32[]{:S(2)}) collective-permute-start(f32[2,1152]{1,0:T(2,128)S(1)} %copy.20), channel_id=1, source_target_pairs={{0,32},{32,64},{64,96},{96,128},{128,160},{160,192},{192,224},{224... | collective-permute-start | bytes 27656 | tf_op jit(solution)/shard_map/while/body/eval_jaxpr/ppermute | solution.py:12
  365.8 11.1 %collective-permute-start = (f32[2,1152]{1,0:T(2,128)S(1)}, f32[2,1152]{1,0:T(2,128)S(1)}, u32[]{:S(2)}, u32[]{:S(2)}) collective-permute-start(f32[2,1152]{1,0:T(2,128)S(1)} %copy.20), channel_id=1, source_target_pairs={{0,32},{32,64},{64,96},{96,128},{128,160},{160,192},{192,224},{224... | collective-permute-start | bytes 27656 | tf_op jit(solution)/shard_map/while/body/eval_jaxpr/ppermute | solution.py:12
  376.9 11.1 %collective-permute-start = (f32[2,1152]{1,0:T(2,128)S(1)}, f32[2,1152]{1,0:T(2,128)S(1)}, u32[]{:S(2)}, u32[]{:S(2)}) collective-permute-start(f32[2,1152]{1,0:T(2,128)S(1)} %copy.20), channel_id=1, source_target_pairs={{0,32},{32,64},{64,96},{96,128},{128,160},{160,192},{192,224},{224... | collective-permute-start | bytes 27656 | tf_op jit(solution)/shard_map/while/body/eval_jaxpr/ppermute | solution.py:12
  388.0 11.1 %collective-permute-start = (f32[2,1152]{1,0:T(2,128)S(1)}, f32[2,1152]{1,0:T(2,128)S(1)}, u32[]{:S(2)}, u32[]{:S(2)}) collective-permute-start(f32[2,1152]{1,0:T(2,128)S(1)} %copy.20), channel_id=1, source_target_pairs={{0,32},{32,64},{64,96},{96,128},{128,160},{160,192},{192,224},{224... | collective-permute-start | bytes 27656 | tf_op jit(solution)/shard_map/while/body/eval_jaxpr/ppermute | solution.py:12
  391.1 8.0 collective-permute-start.1
  399.1 11.1 %collective-permute-start = (f32[2,1152]{1,0:T(2,128)S(1)}, f32[2,1152]{1,0:T(2,128)S(1)}, u32[]{:S(2)}, u32[]{:S(2)}) collective-permute-start(f32[2,1152]{1,0:T(2,128)S(1)} %copy.20), channel_id=1, source_target_pairs={{0,32},{32,64},{64,96},{96,128},{128,160},{160,192},{192,224},{224... | collective-permute-start | bytes 27656 | tf_op jit(solution)/shard_map/while/body/eval_jaxpr/ppermute | solution.py:12
  421.3 355.5 %all-reduce.54.cloned.1.call-start = ((), (), s32[]{:S(2)}) async-start(), calls=%async_computation.4 | async-start | bytes 344064 | tf_op jit(solution)/shard_map/psum | solution.py:115
  440.2 488.0 %all-reduce.58.cloned.1.call-start = ((), (), s32[]{:S(2)}) async-start(), calls=%async_computation.7 | async-start | bytes 147456 | tf_op jit(solution)/shard_map/psum | solution.py:119
  559.3 531.5 %all-reduce.56.cloned.1.call-start = ((), (), s32[]{:S(2)}) async-start(), calls=%async_computation.5 | async-start | bytes 344064 | tf_op jit(solution)/shard_map/psum | solution.py:115
  (14 other events, 335.0 us)
Sparse Core Ops, SparseCore 0:
  10.1 74.2 all-gather.3
  86.5 67.7 all-gather.5
  156.5 66.9 all-gather.7
  421.4 137.7 reduce-scatter.1
  562.6 214.1 all-reduce.53
  779.8 148.3 all-reduce.57
  931.1 159.5 all-reduce.55
